TPU v7x, 32 devices: a whole 2x2x4 slice. The times are simulated.
32 devices in a mesh: dp: 8 (over z, x), tensor: 4 (over y, core).
Axes of the slice: x: 2, y: 2, z: 4, core: 2. Of those that a mesh axis runs over, the one named last changes fastest.
Arguments:
- activations: bfloat16 [4, 4096, 14336], P(None, 'dp', 'tensor'), may hold values from -6 to 6
- out_grads: bfloat16 [4, 4096, 4096], P(None, 'dp', 'tensor'), may hold values from -6 to 6
- proj_in: bfloat16 [4, 40, 14336], P(None, None, 'tensor'), may hold values from -0.046875 to 0.046875
- proj_out: bfloat16 [4, 40, 4096], P(None, None, 'tensor'), may hold values from -0.09375 to 0.09375
- lengths: int32 [32], P('dp'), may hold values from 16 to 128
- example_ids: int32 [32], P('dp'), may hold values from 0 to 31, each once
- prior_cov: bfloat16 [4, 1600, 1600], P('tensor'), as said below
- damping: float32 [4], P('tensor'), may hold values from 10 to 100
- queries: float32 [4, 64, 1600], P('tensor'), may hold values from -2 to 2
Outputs:
- scores: float32 [32, 64], P('dp')
Inputs may be any that keep to these rules, and one draw needn't show every extreme that they name: Each slot's tokens at positions from lengths on are padding. `example_ids`: a permutation of the examples over the slots. `prior_cov`: symmetric and positive definite.
All inputs are finite; a program needn't handle non-finite values.
Results may differ from a plain program's by a relative error of at most 0.0003.
Values sent between devices are 32-bit elements; how exact they have to be, the bound alone decides.
A program may use at most 128 MiB of HBM per device.

v0:
```python
import jax
import jax.numpy as jnp
from jax import lax
from jax.sharding import PartitionSpec as P

KP = 40


def per_device(
    activations, out_grads, proj_in, proj_out, lengths, example_ids, prior_cov, damping, queries
):
    ex_local = lengths.shape[0]
    seq_len = activations.shape[1] // ex_local
    proj_size = KP * KP
    owner_index = lax.axis_index("tensor")
    live_mask = (jnp.arange(seq_len, dtype=jnp.int32)[None, :] < lengths[:, None]).astype(
        jnp.float32
    )
    in_parts = jnp.einsum("ltf,lkf->ltk", activations, proj_in, preferred_element_type=jnp.float32)
    out_parts = jnp.einsum("ltf,lkf->ltk", out_grads, proj_out, preferred_element_type=jnp.float32)
    in_summed, out_summed = lax.psum((in_parts, out_parts), "tensor")
    in_rows = lax.dynamic_index_in_dim(in_summed, owner_index, 0, keepdims=False)
    out_rows = lax.dynamic_index_in_dim(out_summed, owner_index, 0, keepdims=False)
    in_rows = in_rows.reshape(ex_local, seq_len, KP) * live_mask[:, :, None]
    out_rows = out_rows.reshape(ex_local, seq_len, KP)
    proj_grads = jnp.einsum(
        "est,esu->etu", out_rows, in_rows, precision=lax.Precision.HIGHEST
    ).reshape(ex_local, proj_size)
    piece_rows = lax.all_gather(proj_grads, "dp", axis=0, tiled=True)
    moment = jnp.dot(piece_rows.T, piece_rows, precision=lax.Precision.HIGHEST)
    examples_total = ex_local * lax.axis_size("dp")
    covariance = (
        prior_cov[0].astype(jnp.float32)
        + moment / examples_total
        + damping[0] * jnp.eye(proj_size, dtype=jnp.float32)
    )
    factor_lower = jnp.linalg.cholesky(covariance)
    forward_part = lax.linalg.triangular_solve(
        factor_lower, queries[0].T, left_side=True, lower=True
    )
    solved = lax.linalg.triangular_solve(
        factor_lower, forward_part, left_side=True, lower=True, transpose_a=True
    )
    layer_scores = jnp.dot(proj_grads, solved, precision=lax.Precision.HIGHEST)
    slot_scores = lax.psum(layer_scores, "tensor")
    one_hot = (example_ids[:, None] == jnp.arange(examples_total, dtype=jnp.int32)[None, :]).astype(
        jnp.float32
    )
    placed = jnp.einsum("se,sq->eq", one_hot, slot_scores, precision=lax.Precision.HIGHEST)
    return lax.psum_scatter(placed, "dp", scatter_dimension=0, tiled=True)


def solution(mesh):
    in_specs = (
        P(None, "dp", "tensor"),
        P(None, "dp", "tensor"),
        P(None, None, "tensor"),
        P(None, None, "tensor"),
        P("dp"),
        P("dp"),
        P("tensor", None, None),
        P("tensor"),
        P("tensor", None, None),
    )
    out_specs = P("dp", None)
    return jax.shard_map(
        per_device, mesh=mesh, in_specs=in_specs, out_specs=out_specs, check_vma=False
    )
```

profile of v0, /device:TPU:0, one launch (start us, length us, event | category | flops | bytes accessed | tf_op | source)
XLA Modules:
  0.0 746.8 jit_solution(4929965995633981686)
XLA Ops:
  7.9 10.3 %fusion.168 = f32[4,512,40]{1,2,0:T(8,128)} fusion(bf16[4,512,3584]{2,1,0:T(8,128)(2,1)} %param.9, bf16[4,40,3584]{2,1,0:T(8,128)(2,1)S(1)} %copy-done), kind=kOutput, calls=%fused_computation.432 | convolution fusion | flops 587202560 | bytes 16154624 | tf_op jit(solution)/shard_map/ltf,lkf->ltk/dot_general | solution.py:19
  18.2 4.3 fusion.167
  24.5 34.7 %all-reduce.7.cloned.1.call-done = (f32[4,512,40]{1,2,0:T(8,128)}, f32[4,512,40]{1,2,0:T(8,128)}) async-done(((f32[4,512,40]{1,2,0:T(8,128)}, f32[4,512,40]{1,2,0:T(8,128)}), (f32[4,512,40]{1,2,0:T(8,128)}, f32[4,512,40]{1,2,0:T(8,128)})) %all-reduce.7.cloned.1.call-update) | async-done | bytes 655376 | tf_op jit(solution)/shard_map/psum | solution.py:21
  60.8 30.7 %all-gather = f32[8,4,1600]{2,1,0:T(4,128)S(1)} all-gather(f32[1,4,1600]{2,1,0:T(4,128)S(1)} %reshape.205), channel_id=1, replica_groups=mesh['dp'=8,'tensor'=4] {'dp'}, dimensions={0}, use_global_device_ids=true | all-gather | bytes 230400 | tf_op jit(solution)/shard_map/all_gather | solution.py:29
  91.6 16.0 %fusion = f32[1600,1600]{1,0:T(8,128)} fusion(f32[32,1600]{1,0:T(8,128)S(1)} %reshape.206, bf16[1,1600,1600]{2,1,0:T(8,128)(2,1)} %param.15, f32[]{:T(128)} %bitcast.238), kind=kOutput, calls=%fused_computation.4 | convolution fusion | flops 998400000 | bytes 15564804 | tf_op jit(solution)/shard_map/dot_general | solution.py:30
  107.6 13.2 %copy.16 = f32[1600,1600]{0,1:T(8,128)} copy(f32[1600,1600]{1,0:T(8,128)} %fusion) | data formatting | bytes 20480000 | tf_op jit(solution)/shard_map/add | solution.py:33
  120.7 7.9 %fusion.1 = f32[1600,1600]{1,0:T(8,128)S(1)} fusion(f32[1600,1600]{1,0:T(8,128)} %fusion, f32[1600,1600]{0,1:T(8,128)} %copy.16), kind=kLoop, calls=%fused_computation.6 | loop fusion | flops 5120000 | bytes 30720000 | tf_op jit(solution)/shard_map/jit(cholesky)/div | solution.py:37
  128.7 4.0 copy-done.3
  132.7 11.7 %cholesky.371 = f32[128,128]{1,0:T(8,128)S(1)} custom-call(f32[128,128]{1,0:T(8,128)S(1)} %cholesky.973), custom_call_target="Cholesky" | custom-call | tf_op jit(solution)/shard_map/jit(cholesky)/cholesky | solution.py:37
  144.5 4.6 cholesky.401
  149.0 9.8 %custom-call.104 = f32[1,128,128]{1,2,0:T(8,128)S(1)} custom-call(f32[1,128,128]{2,1,0:T(8,128)S(1)} %get-tuple-element.59), custom_call_target="InvertDiagBlocksLowerTriangular" | custom-call | tf_op jit(solution)/shard_map/jit(cholesky)/cholesky | solution.py:37
  158.8 2.8 constant_dynamic-update-slice_fusion.160
  163.5 11.7 %cholesky.390 = f32[128,128]{1,0:T(8,128)S(1)} custom-call(f32[128,128]{1,0:T(8,128)S(1)} %cholesky.977), custom_call_target="Cholesky" | custom-call | tf_op jit(solution)/shard_map/jit(cholesky)/cholesky | solution.py:37
  175.9 10.2 %custom-call.105 = f32[1,128,128]{1,2,0:T(8,128)S(1)} custom-call(f32[1,128,128]{2,1,0:T(8,128)S(1)} %get-tuple-element.56), custom_call_target="InvertDiagBlocksLowerTriangular" | custom-call | tf_op jit(solution)/shard_map/jit(cholesky)/cholesky | solution.py:37
  187.6 2.8 convolution_subtract_fusion.2
  190.5 11.7 %cholesky.415 = f32[128,128]{1,0:T(8,128)S(1)} custom-call(f32[128,128]{1,0:T(8,128)S(1)} %cholesky.982), custom_call_target="Cholesky" | custom-call | tf_op jit(solution)/shard_map/jit(cholesky)/cholesky | solution.py:37
  202.9 9.8 %custom-call.106 = f32[1,128,128]{1,2,0:T(8,128)S(1)} custom-call(f32[1,128,128]{2,1,0:T(8,128)S(1)} %get-tuple-element.53), custom_call_target="InvertDiagBlocksLowerTriangular" | custom-call | tf_op jit(solution)/shard_map/jit(cholesky)/cholesky | solution.py:37
  214.2 3.6 convolution_subtract_fusion.1
  217.9 11.7 %cholesky.772 = f32[128,128]{1,0:T(8,128)S(1)} custom-call(f32[128,128]{1,0:T(8,128)S(1)} %cholesky.987), custom_call_target="Cholesky" | custom-call | tf_op jit(solution)/shard_map/jit(cholesky)/cholesky | solution.py:37
  230.3 9.8 %custom-call.107 = f32[1,128,128]{1,2,0:T(8,128)S(1)} custom-call(f32[1,128,128]{2,1,0:T(8,128)S(1)} %get-tuple-element.50), custom_call_target="InvertDiagBlocksLowerTriangular" | custom-call | tf_op jit(solution)/shard_map/jit(cholesky)/cholesky | solution.py:37
  241.6 3.7 convolution_subtract_fusion
  245.3 11.9 %cholesky.791 = f32[128,128]{1,0:T(8,128)S(1)} custom-call(f32[128,128]{1,0:T(8,128)S(1)} %cholesky.992), custom_call_target="Cholesky" | custom-call | tf_op jit(solution)/shard_map/jit(cholesky)/cholesky | solution.py:37
  257.9 9.8 %custom-call.108 = f32[1,128,128]{1,2,0:T(8,128)S(1)} custom-call(f32[1,128,128]{2,1,0:T(8,128)S(1)} %get-tuple-element.47), custom_call_target="InvertDiagBlocksLowerTriangular" | custom-call | tf_op jit(solution)/shard_map/jit(cholesky)/cholesky | solution.py:37
  269.1 4.0 fusion.17
  273.1 11.7 %cholesky.811 = f32[128,128]{1,0:T(8,128)S(1)} custom-call(f32[128,128]{1,0:T(8,128)S(1)} %cholesky.997), custom_call_target="Cholesky" | custom-call | tf_op jit(solution)/shard_map/jit(cholesky)/cholesky | solution.py:37
  285.4 9.8 %custom-call.109 = f32[1,128,128]{1,2,0:T(8,128)S(1)} custom-call(f32[1,128,128]{2,1,0:T(8,128)S(1)} %get-tuple-element.44), custom_call_target="InvertDiagBlocksLowerTriangular" | custom-call | tf_op jit(solution)/shard_map/jit(cholesky)/cholesky | solution.py:37
  296.9 4.0 fusion.20
  301.0 11.7 %cholesky.831 = f32[128,128]{1,0:T(8,128)S(1)} custom-call(f32[128,128]{1,0:T(8,128)S(1)} %cholesky.1002), custom_call_target="Cholesky" | custom-call | tf_op jit(solution)/shard_map/jit(cholesky)/cholesky | solution.py:37
  313.4 9.8 %custom-call.110 = f32[1,128,128]{1,2,0:T(8,128)S(1)} custom-call(f32[1,128,128]{2,1,0:T(8,128)S(1)} %get-tuple-element.41), custom_call_target="InvertDiagBlocksLowerTriangular" | custom-call | tf_op jit(solution)/shard_map/jit(cholesky)/cholesky | solution.py:37
  324.4 4.0 fusion.23
  328.5 11.9 %cholesky.851 = f32[128,128]{1,0:T(8,128)S(1)} custom-call(f32[128,128]{1,0:T(8,128)S(1)} %cholesky.1007), custom_call_target="Cholesky" | custom-call | tf_op jit(solution)/shard_map/jit(cholesky)/cholesky | solution.py:37
  341.0 9.8 %custom-call.111 = f32[1,128,128]{1,2,0:T(8,128)S(1)} custom-call(f32[1,128,128]{2,1,0:T(8,128)S(1)} %get-tuple-element.38), custom_call_target="InvertDiagBlocksLowerTriangular" | custom-call | tf_op jit(solution)/shard_map/jit(cholesky)/cholesky | solution.py:37
  352.0 3.8 fusion.26
  355.8 11.7 %cholesky.871 = f32[128,128]{1,0:T(8,128)S(1)} custom-call(f32[128,128]{1,0:T(8,128)S(1)} %cholesky.1012), custom_call_target="Cholesky" | custom-call | tf_op jit(solution)/shard_map/jit(cholesky)/cholesky | solution.py:37
  368.2 10.2 %custom-call.112 = f32[1,128,128]{1,2,0:T(8,128)S(1)} custom-call(f32[1,128,128]{2,1,0:T(8,128)S(1)} %get-tuple-element.35), custom_call_target="InvertDiagBlocksLowerTriangular" | custom-call | tf_op jit(solution)/shard_map/jit(cholesky)/cholesky | solution.py:37
  379.5 3.6 fusion.29
  383.1 11.7 %cholesky.891 = f32[128,128]{1,0:T(8,128)S(1)} custom-call(f32[128,128]{1,0:T(8,128)S(1)} %cholesky.1017), custom_call_target="Cholesky" | custom-call | tf_op jit(solution)/shard_map/jit(cholesky)/cholesky | solution.py:37
  395.4 9.8 %custom-call.113 = f32[1,128,128]{1,2,0:T(8,128)S(1)} custom-call(f32[1,128,128]{2,1,0:T(8,128)S(1)} %get-tuple-element.32), custom_call_target="InvertDiagBlocksLowerTriangular" | custom-call | tf_op jit(solution)/shard_map/jit(cholesky)/cholesky | solution.py:37
  406.2 3.1 fusion.32
  409.3 11.9 %cholesky.911 = f32[128,128]{1,0:T(8,128)S(1)} custom-call(f32[128,128]{1,0:T(8,128)S(1)} %cholesky.1022), custom_call_target="Cholesky" | custom-call | tf_op jit(solution)/shard_map/jit(cholesky)/cholesky | solution.py:37
  421.8 9.8 %custom-call.114 = f32[1,128,128]{1,2,0:T(8,128)S(1)} custom-call(f32[1,128,128]{2,1,0:T(8,128)S(1)} %get-tuple-element.29), custom_call_target="InvertDiagBlocksLowerTriangular" | custom-call | tf_op jit(solution)/shard_map/jit(cholesky)/cholesky | solution.py:37
  432.5 2.5 convolution_subtract_fusion.4
  435.1 11.7 %cholesky.931 = f32[128,128]{1,0:T(8,128)S(1)} custom-call(f32[128,128]{1,0:T(8,128)S(1)} %cholesky.1027), custom_call_target="Cholesky" | custom-call | tf_op jit(solution)/shard_map/jit(cholesky)/cholesky | solution.py:37
  447.5 9.8 %custom-call.115 = f32[1,128,128]{1,2,0:T(8,128)S(1)} custom-call(f32[1,128,128]{2,1,0:T(8,128)S(1)} %get-tuple-element.26), custom_call_target="InvertDiagBlocksLowerTriangular" | custom-call | tf_op jit(solution)/shard_map/jit(cholesky)/cholesky | solution.py:37
  459.7 5.8 cholesky.952
  483.0 4.8 select_select_fusion
  487.8 4.0 copy-done.2
  491.8 33.7 %while.1 = (s32[]{:T(128)}, f32[1600,1600]{1,0:T(8,128)}, s32[12,2]{0,1:T(2,128)S(1)}, f32[12,128,128]{2,1,0:T(8,128)S(1)}, s32[]{:T(128)}) while((s32[]{:T(128)}, f32[1600,1600]{1,0:T(8,128)}, s32[12,2]{0,1:T(2,128)S(1)}, f32[12,128,128]{2,1,0:T(8,128)S(1)}, s32[]{:T(128)}) %tuple.127), condition=%wide.while_cond, body=%wide.while_body.sunk | while | flops 2 | bytes 131189 | solution.py:41
  492.4 2.2 bitcast_dynamic-update-slice_fusion.2
  495.2 2.2 bitcast_dynamic-update-slice_fusion.2
  498.0 2.2 bitcast_dynamic-update-slice_fusion.2
  500.8 2.2 bitcast_dynamic-update-slice_fusion.2
  503.6 2.2 bitcast_dynamic-update-slice_fusion.2
  506.5 2.2 bitcast_dynamic-update-slice_fusion.2
  509.3 2.2 bitcast_dynamic-update-slice_fusion.2
  512.1 2.2 bitcast_dynamic-update-slice_fusion.2
  514.9 2.2 bitcast_dynamic-update-slice_fusion.2
  517.7 2.2 bitcast_dynamic-update-slice_fusion.2
  520.5 2.2 bitcast_dynamic-update-slice_fusion.2
  523.3 2.2 bitcast_dynamic-update-slice_fusion.2
  525.7 127.9 %custom-call.116 = f32[13,128,128]{1,2,0:T(8,128)S(1)} custom-call(f32[13,128,128]{2,1,0:T(8,128)S(1)} %pad_maximum_fusion), custom_call_target="InvertDiagBlocksLowerTriangular" | custom-call | tf_op jit(solution)/shard_map/triangular_solve | solution.py:41
  670.9 2.0 convolution_subtract_fusion.15
  696.1 5.9 psum.23
  702.3 36.8 %all-reduce.3 = f32[32,64]{1,0:T(8,128)S(1)} all-reduce(f32[32,64]{1,0:T(8,128)S(1)} %fusion.157), channel_id=2, replica_groups=mesh['dp'=8,'tensor'=4] {'dp'}, use_global_device_ids=true, to_apply=%region_29.30.clone | all-reduce | flops 2048 | bytes 16384
  (236 shorter events, 85.3 us)
Async XLA Ops:
  6.5 1.4 copy-start
  6.5 16.6 %copy-start.8 = (u32[32]{0:T(128)S(1)}, u32[32]{0:T(128)}, u32[]{:S(2)}) copy-start(u32[32]{0:T(128)} %constant.497) | copy-start | bytes 388
  6.5 11.6 %copy-start.5 = (bf16[4,40,1024]{2,1,0:T(8,128)(2,1)S(1)}, bf16[4,40,1024]{2,1,0:T(8,128)(2,1)}, u32[]{:S(2)}) copy-start(bf16[4,40,1024]{2,1,0:T(8,128)(2,1)} %param.12) | copy-start | bytes 983044
  6.5 17.9 %copy-start.6 = (s32[4]{0:T(128)S(1)}, s32[4]{0:T(128)}, u32[]{:S(2)}) copy-start(s32[4]{0:T(128)} %param.13) | copy-start | bytes 52
  6.5 52.7 %all-reduce.7.cloned.1.call-start = ((), (), s32[]{:S(2)}) async-start(), calls=%async_computation | async-start | bytes 1310720 | tf_op jit(solution)/shard_map/psum | solution.py:21
  128.7 4.0 copy-start.3
  483.0 170.6 %copy-start.4 = (f32[1,64,1600]{2,1,0:T(8,128)S(1)}, f32[1,64,1600]{2,1,0:T(8,128)}, u32[]{:S(2)}) copy-start(f32[1,64,1600]{2,1,0:T(8,128)} %param.17) | copy-start | bytes 1228804
  487.8 4.0 copy-start.2
  664.6 75.0 %copy-start.1 = (bf16[4,40,3584]{2,1,0:T(8,128)(2,1)S(1)}, bf16[4,40,3584]{2,1,0:T(8,128)(2,1)}, u32[]{:S(2)}) copy-start(bf16[4,40,3584]{2,1,0:T(8,128)(2,1)} %param.11) | copy-start | bytes 3440644
  664.6 37.4 %copy-start.7 = (s32[4]{0:T(128)S(1)}, s32[4]{0:T(128)}, u32[]{:S(2)}) copy-start(s32[4]{0:T(128)} %param.14) | copy-start | bytes 52
Sparse Core Ops, SparseCore 0:
  22.6 36.6 all-reduce.6
where the time goes:
time: 757 us; the launch traced here: 747 us
  other arithmetic  423 us (56%)
  matrix products  128 us (17%)
  blocking collectives  73.4 us (10%)
  local copies, waits for them, and re-layouts  63.5 us (8%)
  waiting for transfers between devices  34.7 us (5%)
  between operations  24.6 us (3%)
    another operation x51, other arithmetic, per_device(): factor_lower = jnp.linalg.cholesky(covariance)  282 us
    another operation x7, other arithmetic, per_device(): lax.linalg.triangular_solve(factor_lower, forward_part, left_side=True, l...  133 us
    another operation x24, matrix products, per_device(): factor_lower = jnp.linalg.cholesky(covariance)  55.4 us
    unnamed x1, blocking collectives  36.8 us
    psum x1, waiting for transfers between devices, per_device(): in_summed, out_summed = lax.psum((in_parts, out_parts), 'tensor')  34.7 us
    another operation x36, local copies, waits for them, and re-layouts  33.5 us
    all_gather x1, blocking collectives, per_device(): piece_rows = lax.all_gather(proj_grads, 'dp', axis=0, tiled=True)  30.7 us
    another operation x25, matrix products, per_device(): lax.linalg.triangular_solve(factor_lower, queries[0].T, left_side=True, l...  21 us
  transfers between devices with their start and end apart: 1, of which 1 were waited for; matrix products, arithmetic and copies ran while one was open for 0% of the time, Pallas kernels for 0%

commit v1 on v0

v1 whole, which is shorter than its diff:
```python
import functools

import jax
import jax.numpy as jnp
from jax import lax
from jax.experimental import pallas as pl
from jax.experimental.pallas import tpu as pltpu
from jax.sharding import PartitionSpec as P

NB = 128
CB = 256


def round_up(value, step):
    return -(-value // step) * step


def split3(x):
    high = x.astype(jnp.bfloat16)
    rest = x - high.astype(jnp.float32)
    mid = rest.astype(jnp.bfloat16)
    low = (rest - mid.astype(jnp.float32)).astype(jnp.bfloat16)
    return high, mid, low


def stack_left(x):
    h, m, l = split3(x)
    return jnp.concatenate([h, h, m, h, l, m], axis=1)


def stack_right(x):
    h, m, l = split3(x)
    return jnp.concatenate([h, m, h, l, h, m], axis=1)


def dot_nt(a, b):
    return lax.dot_general(a, b, (((1,), (1,)), ((), ())), preferred_element_type=jnp.float32)


def across(row, shape=(8, NB)):
    return jnp.broadcast_to(row, shape)


def invert_block(rows):
    sub = lax.broadcasted_iota(jnp.int32, (8, NB), 0)
    lane = lax.broadcasted_iota(jnp.int32, (8, NB), 1)
    count = len(rows)
    for kb in range(count):
        base = 8 * kb
        strip = rows[kb]
        cols = [across(strip[:, base + j : base + j + 1]) for j in range(8)]
        for p in range(8):
            pivot_col = cols[p]
            inv = 1.0 / across(pivot_col[p : p + 1, :])
            new = []
            for j in range(8):
                if j == p:
                    new.append(jnp.where(sub == p, inv, -pivot_col * inv))
                else:
                    lead = across(cols[j][p : p + 1, :])
                    new.append(jnp.where(sub == p, lead * inv, cols[j] - (pivot_col * lead) * inv))
            cols = new
        inside = (lane >= base) & (lane < base + 8)
        strip = jnp.where(inside, jnp.where(lane - base == sub, 1.0, 0.0), strip)
        terms = [cols[j] * across(strip[j : j + 1, :]) for j in range(8)]
        top = ((terms[0] + terms[1]) + (terms[2] + terms[3])) + (
            (terms[4] + terms[5]) + (terms[6] + terms[7])
        )
        spread = [across(top[j : j + 1, :]) for j in range(8)]
        for step in range(1, count):
            i = (kb + step) % count
            row = rows[i]
            parts = [across(row[:, base + j : base + j + 1]) * spread[j] for j in range(8)]
            total = ((parts[0] + parts[1]) + (parts[2] + parts[3])) + (
                (parts[4] + parts[5]) + (parts[6] + parts[7])
            )
            rows[i] = jnp.where(inside, 0.0, row) - total
        rows[kb] = top
    return rows


def solve_kernel(
    size, damping_ref, prior_ref, rhs_ref, lead_ref, out_ref, mat, left, right, dinv
):
    width = rhs_ref.shape[1]
    col_blocks = width // CB
    all_blocks = mat.shape[0]
    slots = lead_ref.shape[2]
    damp = damping_ref[0, 0]

    def fill(i, carry):
        at = pl.multiple_of(i * 16, 16)
        row_id = lax.broadcasted_iota(jnp.int32, (16, CB), 0) + at
        col_id = lax.broadcasted_iota(jnp.int32, (16, CB), 1)
        for jj in range(col_blocks):
            lo, hi = jj * CB, min((jj + 1) * CB, size)
            piece = prior_ref[pl.ds(at, 16), lo:hi].astype(jnp.float32)
            if hi - lo < CB:
                piece = jnp.concatenate(
                    [piece, jnp.zeros((16, CB - (hi - lo)), jnp.float32)], axis=1
                )
            piece = jnp.where(row_id == col_id + lo, piece + damp, piece)
            mat[jj, pl.ds(at, 16), :] = piece
        return carry

    lax.fori_loop(0, size // 16, fill, 0)
    for jj in range(col_blocks):
        row_id = lax.broadcasted_iota(jnp.int32, (width - size, CB), 0) + size
        col_id = lax.broadcasted_iota(jnp.int32, (width - size, CB), 1) + jj * CB
        mat[jj, size:width, :] = jnp.where(row_id == col_id, 1.0, 0.0)
        mat[jj, width:, :] = rhs_ref[:, jj * CB : (jj + 1) * CB]
    mat[col_blocks, width:, :] = jnp.zeros((mat.shape[1] - width, CB), jnp.float32)

    def trail(first):
        def per_col(jj, carry):
            weights = right[pl.ds(pl.multiple_of(jj * CB, CB), CB), :]

            def per_row(r, inner):
                at = pl.multiple_of(r * CB, CB)
                mat[jj, pl.ds(at, CB), :] -= dot_nt(left[pl.ds(at, CB), :], weights)
                return inner

            return lax.fori_loop(jj, all_blocks, per_row, carry)

        lax.fori_loop(first, all_blocks, per_col, 0)

    def lead_rows(r, carry):
        at = pl.multiple_of(r * CB, CB)
        piece = lead_ref[0, pl.ds(at, CB), :]
        right[pl.ds(at, CB), :] = stack_right(piece)
        left[pl.ds(at, CB), :] = stack_left(lead_ref[1, pl.ds(at, CB), :])
        return carry

    lax.fori_loop(0, all_blocks, lead_rows, 0)
    trail(0)

    def step(k, carry):
        half = k // 2
        lanes = pl.ds(pl.multiple_of((k % 2) * NB, NB), NB)
        top = pl.multiple_of(k * NB, NB)
        rows = [mat[half, pl.ds(top + 8 * i, 8), lanes] for i in range(NB // 8)]
        rows = invert_block(rows)
        for i in range(NB // 8):
            dinv[8 * i : 8 * i + 8, :] = rows[i]
        inverse = stack_right(dinv[...])

        def per_row(r, inner):
            at = pl.multiple_of(r * CB, CB)
            panel = mat[half, pl.ds(at, CB), lanes]
            right[pl.ds(at, CB), :] = stack_right(panel)
            left[pl.ds(at, CB), :] = stack_left(dot_nt(stack_left(panel), inverse))
            return inner

        lax.fori_loop(half, all_blocks, per_row, 0)
        trail((k + 1) // 2)
        return carry

    lax.fori_loop(0, round_up(size, NB) // NB, step, 0)
    out_ref[...] = -mat[col_blocks, width:, :]


def solve_scores(prior, damping, queries, grads):
    slots, size = grads.shape
    asked = queries.shape[0]
    width = round_up(size, CB)
    extra = CB
    rows = width + extra
    rhs = jnp.concatenate([grads, queries], axis=0)
    rhs = jnp.pad(rhs, ((0, extra - slots - asked), (0, width - size)))
    lead = jnp.pad(grads.T, ((0, rows - size), (0, NB - slots)))
    lead = jnp.stack([lead, lead * (-1.0 / slots)])
    out = pl.pallas_call(
        functools.partial(solve_kernel, size),
        out_shape=jax.ShapeDtypeStruct((extra, CB), jnp.float32),
        in_specs=[
            pl.BlockSpec(memory_space=pltpu.SMEM),
            pl.BlockSpec(memory_space=pltpu.VMEM),
            pl.BlockSpec(memory_space=pltpu.VMEM),
            pl.BlockSpec(memory_space=pltpu.VMEM),
        ],
        out_specs=pl.BlockSpec(memory_space=pltpu.VMEM),
        scratch_shapes=[
            pltpu.VMEM((rows // CB, rows, CB), jnp.float32),
            pltpu.VMEM((rows, 6 * NB), jnp.bfloat16),
            pltpu.VMEM((rows, 6 * NB), jnp.bfloat16),
            pltpu.VMEM((NB, NB), jnp.float32),
        ],
        compiler_params=pltpu.CompilerParams(vmem_limit_bytes=56 * 1024 * 1024),
    )(damping.reshape(1, 1), prior, rhs, lead)
    return out[:slots, slots : slots + asked]


def per_device(
    activations, out_grads, proj_in, proj_out, lengths, example_ids, prior_cov, damping, queries
):
    ex_local = lengths.shape[0]
    rank = proj_in.shape[1]
    seq_len = activations.shape[1] // ex_local
    owner_index = lax.axis_index("tensor")
    live_mask = (jnp.arange(seq_len, dtype=jnp.int32)[None, :] < lengths[:, None]).astype(
        jnp.float32
    )
    in_parts = jnp.einsum("ltf,lkf->ltk", activations, proj_in, preferred_element_type=jnp.float32)
    out_parts = jnp.einsum("ltf,lkf->ltk", out_grads, proj_out, preferred_element_type=jnp.float32)
    in_summed, out_summed = lax.psum((in_parts, out_parts), "tensor")
    in_rows = lax.dynamic_index_in_dim(in_summed, owner_index, 0, keepdims=False)
    out_rows = lax.dynamic_index_in_dim(out_summed, owner_index, 0, keepdims=False)
    in_rows = in_rows.reshape(ex_local, seq_len, rank) * live_mask[:, :, None]
    out_rows = out_rows.reshape(ex_local, seq_len, rank)
    proj_grads = jnp.einsum(
        "est,esu->etu", out_rows, in_rows, precision=lax.Precision.HIGHEST
    ).reshape(ex_local, rank * rank)
    ids = lax.all_gather(example_ids, "dp", axis=0, tiled=True)
    piece_rows = lax.all_gather(proj_grads, "dp", axis=0, tiled=True)
    scores = solve_scores(prior_cov[0], damping, queries[0], piece_rows)
    mine = lax.axis_index("dp") * ex_local + jnp.arange(ex_local, dtype=jnp.int32)
    pick = (ids[None, :] == mine[:, None]).astype(jnp.float32)
    chosen = jnp.dot(pick, scores, precision=lax.Precision.HIGHEST)
    return lax.psum(chosen, "tensor")


def solution(mesh):
    in_specs = (
        P(None, "dp", "tensor"),
        P(None, "dp", "tensor"),
        P(None, None, "tensor"),
        P(None, None, "tensor"),
        P("dp"),
        P("dp"),
        P("tensor", None, None),
        P("tensor"),
        P("tensor", None, None),
    )
    out_specs = P("dp", None)
    return jax.shard_map(
        per_device, mesh=mesh, in_specs=in_specs, out_specs=out_specs, check_vma=False
    )
```

time: 757 us -> 259 us (0.34); the launches traced: 747 us -> 259 us
  other arithmetic: 423 us -> 3.03 us
  Pallas kernels: 0 us -> 150 us
  matrix products: 128 us -> 15.9 us
  local copies, waits for them, and re-layouts: 63.5 us -> 2.89 us
  blocking collectives: 73.4 us -> 50.3 us
  waiting for transfers between devices: 34.7 us -> 21.5 us
  between operations: 24.6 us -> 14.8 us
    another operation x58 -> x2, other arithmetic: 415 us -> 1.6 us  [solve_scores(): lead = jnp.stack([lead, lead * (-1.0 / slots)])]
    pallas_call x0 -> x1, Pallas kernels: none -> 150 us  [solve_scores(): pl.pallas_call(functools.partial(solve_kernel, size), out_shape=jax.Shape...]
    another operation x74 -> x0, matrix products: 96.2 us -> none  [the longest x24 55.4 us: per_device(): factor_lower = jnp.linalg.cholesky(covariance)]
    another operation x60 -> x0, local copies, waits for them, and re-layouts: 38.1 us -> none
    unnamed x1, blocking collectives: 36.8 us -> 13.1 us
    dot_general x3 -> x1, matrix products: 16.7 us -> 0.9 us  [per_device(): chosen = jnp.dot(pick, scores, precision=lax.Precision.HIGHEST)]
    psum x1, waiting for transfers between devices: 34.7 us -> 21.5 us  [per_device(): in_summed, out_summed = lax.psum((in_parts, out_parts), 'tensor')]
    add x1 -> x0, local copies, waits for them, and re-layouts: 13.2 us -> none  [per_device(): prior_cov[0].astype(jnp.float32) + moment / examples_total]
where the time goes in v1:
time: 259 us
  Pallas kernels  150 us (58%)
  blocking collectives  50.3 us (19%)
  waiting for transfers between devices  21.5 us (8%)
  matrix products  15.9 us (6%)
  between operations  14.8 us (6%)
  other arithmetic  3.03 us (1%)
  local copies, waits for them, and re-layouts  2.89 us (1%)
    pallas_call x1, Pallas kernels, solve_scores(): pl.pallas_call(functools.partial(solve_kernel, size), out_shape=jax.Shape...  150 us
    all_gather x1, blocking collectives, per_device(): piece_rows = lax.all_gather(proj_grads, 'dp', axis=0, tiled=True)  30.7 us
    psum x1, waiting for transfers between devices, per_device(): in_summed, out_summed = lax.psum((in_parts, out_parts), 'tensor')  21.5 us
    unnamed x1, blocking collectives  13.1 us
    dot_general x1, matrix products, per_device(): jnp.einsum('ltf,lkf->ltk', activations, proj_in, preferred_element_type=j...  10.3 us
    psum x1, blocking collectives, per_device(): return lax.psum(chosen, 'tensor')  6.48 us
  transfers between devices with their start and end apart: 1, of which 1 were waited for; matrix products, arithmetic and copies ran while one was open for 0% of the time, Pallas kernels for 0%

profile of v1, /device:TPU:0, one launch (start us, length us, event | category | flops | bytes accessed | tf_op | source)
XLA Modules:
  0.0 258.8 jit_solution(3463711896132362425)
XLA Ops:
  6.5 0.0 copy-start
  6.5 0.0 all-reduce.6.cloned.1.call-start
  6.5 4.4 %fusion.10 = f32[4,512,40]{1,2,0:T(8,128)} fusion(bf16[4,512,1024]{2,1,0:T(8,128)(2,1)} %param.10, bf16[4,40,1024]{2,1,0:T(8,128)(2,1)} %param.12), kind=kOutput, calls=%fused_computation.21 | convolution fusion | flops 167772160 | bytes 4849664 | tf_op jit(solution)/shard_map/ltf,lkf->ltk/dot_general | solution.py:204
  11.0 0.0 copy-done
  11.0 0.0 copy-start.4
  11.0 0.0 copy-start.3
  11.0 0.0 copy-start.2
  11.0 10.3 %fusion.11 = f32[4,512,40]{1,2,0:T(8,128)} fusion(bf16[4,512,3584]{2,1,0:T(8,128)(2,1)} %param.9, bf16[4,40,3584]{2,1,0:T(8,128)(2,1)S(1)} %copy-done), kind=kOutput, calls=%fused_computation.22 | convolution fusion | flops 587202560 | bytes 16154624 | tf_op jit(solution)/shard_map/ltf,lkf->ltk/dot_general | solution.py:203
  21.3 0.0 all-reduce.6.cloned.1.call-update
  22.0 0.0 copy-done.4
  22.0 0.6 dynamic-slice
  23.2 0.0 copy-done.3
  23.2 0.2 dynamic-update-slice
  23.5 13.1 %all-reduce.2 = s32[32]{0:T(128)S(1)} all-reduce(s32[32]{0:T(128)S(1)} %dynamic-update-slice), channel_id=1, replica_groups=mesh['dp'=8,'tensor'=4] {'dp'}, use_global_device_ids=true, to_apply=%add.2 | all-reduce | flops 32 | bytes 256
  36.5 0.0 copy-done.2
  36.5 0.1 fusion.6
  36.6 21.5 %all-reduce.6.cloned.1.call-done = (f32[4,512,40]{1,2,0:T(8,128)}, f32[4,512,40]{1,2,0:T(8,128)}) async-done(((f32[4,512,40]{1,2,0:T(8,128)}, f32[4,512,40]{1,2,0:T(8,128)}), (f32[4,512,40]{1,2,0:T(8,128)}, f32[4,512,40]{1,2,0:T(8,128)})) %all-reduce.6.cloned.1.call-update) | async-done | bytes 655376 | tf_op jit(solution)/shard_map/psum | solution.py:205
  58.1 0.9 constant_dynamic-slice_fusion
  59.1 0.3 fusion.1
  59.4 0.1 reshape.48
  59.5 30.7 %all-gather = f32[8,4,1600]{2,1,0:T(4,128)S(1)} all-gather(f32[1,4,1600]{2,1,0:T(4,128)S(1)} %reshape.48), channel_id=1, replica_groups=mesh['dp'=8,'tensor'=4] {'dp'}, dimensions={0}, use_global_device_ids=true | all-gather | bytes 230400 | tf_op jit(solution)/shard_map/all_gather | solution.py:214
  90.2 0.1 reshape.49
  90.3 0.0 copy-start.1
  90.3 0.3 copy.17
  90.6 0.1 pad_bitcast_fusion
  90.8 0.6 copy-done.1
  91.3 1.3 select_maximum_fusion.rhs_ref
  92.7 1.5 pad_maximum_fusion.lead_ref
  94.1 150.4 %shard_map.91 = f32[256,256]{1,0:T(8,128)} custom-call(f32[1,1]{1,0:T(1,128)} %bitcast.20.damping_ref, bf16[1600,1600]{1,0:T(8,128)(2,1)} %bitcast.21, f32[256,1792]{1,0:T(8,128)} %select_maximum_fusion.rhs_ref, f32[2,2048,128]{2,1,0:T(8,128)} %pad_maximum_fusion.lead_ref), custom_call_target="tpu_custom_call" | custom-call | tf_op jit(solution)/shard_map/pallas_call | solution.py:172
  244.5 0.9 fusion.4
  245.4 6.5 %psum.23 = f32[4,64]{1,0:T(4,128)} all-reduce(f32[4,64]{1,0:T(4,128)S(1)} %fusion.4), channel_id=1, replica_groups=mesh['dp'=8,'tensor'=4] {'tensor'}, use_global_device_ids=true, to_apply=%region_2.3 | all-reduce | flops 256 | bytes 2048 | tf_op jit(solution)/shard_map/psum | solution.py:219
  (6 shorter events, 0.1 us)
Async XLA Ops:
  6.5 4.4 %copy-start = (bf16[4,40,3584]{2,1,0:T(8,128)(2,1)S(1)}, bf16[4,40,3584]{2,1,0:T(8,128)(2,1)}, u32[]{:S(2)}) copy-start(bf16[4,40,3584]{2,1,0:T(8,128)(2,1)} %param.11) | copy-start | bytes 3440644
  6.5 51.5 %all-reduce.6.cloned.1.call-start = ((), (), s32[]{:S(2)}) async-start(), calls=%async_computation | async-start | bytes 1310720 | tf_op jit(solution)/shard_map/psum | solution.py:205
  11.0 11.0 %copy-start.4 = (u32[32]{0:T(128)S(1)}, u32[32]{0:T(128)}, u32[]{:S(2)}) copy-start(u32[32]{0:T(128)} %constant.34) | copy-start | bytes 388
  11.0 12.3 %copy-start.3 = (s32[4]{0:T(128)S(1)}, s32[4]{0:T(128)}, u32[]{:S(2)}) copy-start(s32[4]{0:T(128)} %param.14) | copy-start | bytes 52
  11.0 25.6 %copy-start.2 = (s32[4]{0:T(128)S(1)}, s32[4]{0:T(128)}, u32[]{:S(2)}) copy-start(s32[4]{0:T(128)} %param.13) | copy-start | bytes 52
  90.3 1.0 copy-start.1
Sparse Core Ops, SparseCore 0:
  21.4 36.6 all-reduce.5

commit v2 on v1

--- a/solution.py
+++ b/solution.py
@@ -7,8 +7,10 @@
 from jax.experimental.pallas import tpu as pltpu
 from jax.sharding import PartitionSpec as P
 
+MESH = pl.DeviceIdType.MESH
 NB = 128
 CB = 256
+TERMS = 6
 
 
 def round_up(value, step):
@@ -80,12 +82,11 @@
 
 
 def solve_kernel(
-    size, damping_ref, prior_ref, rhs_ref, lead_ref, out_ref, mat, left, right, dinv
+    size, slots, asked, ex_local, damping_ref, prior_ref, rhs_ref, out_ref, mat, left, right, dinv
 ):
     width = rhs_ref.shape[1]
     col_blocks = width // CB
     all_blocks = mat.shape[0]
-    slots = lead_ref.shape[2]
     damp = damping_ref[0, 0]
 
     def fill(i, carry):
@@ -124,14 +125,13 @@
 
         lax.fori_loop(first, all_blocks, per_col, 0)
 
-    def lead_rows(r, carry):
-        at = pl.multiple_of(r * CB, CB)
-        piece = lead_ref[0, pl.ds(at, CB), :]
-        right[pl.ds(at, CB), :] = stack_right(piece)
-        left[pl.ds(at, CB), :] = stack_left(lead_ref[1, pl.ds(at, CB), :])
-        return carry
-
-    lax.fori_loop(0, all_blocks, lead_rows, 0)
+    live = lax.broadcasted_iota(jnp.int32, (NB, CB), 0) < slots
+    for jj in range(col_blocks):
+        piece = jnp.where(live, rhs_ref[0:NB, jj * CB : (jj + 1) * CB], 0.0).T
+        right[jj * CB : (jj + 1) * CB, :] = stack_right(piece)
+        left[jj * CB : (jj + 1) * CB, :] = stack_left(piece * (-1.0 / slots))
+    right[width:, :] = jnp.zeros((mat.shape[1] - width, TERMS * NB), jnp.bfloat16)
+    left[width:, :] = jnp.zeros((mat.shape[1] - width, TERMS * NB), jnp.bfloat16)
     trail(0)
 
     def step(k, carry):
@@ -156,66 +156,222 @@
         return carry
 
     lax.fori_loop(0, round_up(size, NB) // NB, step, 0)
-    out_ref[...] = -mat[col_blocks, width:, :]
-
-
-def solve_scores(prior, damping, queries, grads):
-    slots, size = grads.shape
-    asked = queries.shape[0]
+    id_at = round_up(size, NB)
+    ids = jnp.broadcast_to(rhs_ref[0:slots, id_at : id_at + 1], (slots, NB))
+    own = lax.broadcasted_iota(jnp.int32, (slots, NB), 1) + lax.axis_index("dp") * ex_local
+    pick = jnp.where(ids == own.astype(jnp.float32), -1.0, 0.0)
+    chosen = lax.dot_general(
+        pick,
+        mat[col_blocks, width : width + slots, :],
+        (((0,), (0,)), ((), ())),
+        precision=lax.Precision.HIGHEST,
+        preferred_element_type=jnp.float32,
+    )
+    out_ref[...] = chosen[0:ex_local, slots : slots + asked]
+
+
+def project_kernel(
+    ex_local,
+    size,
+    act_hbm,
+    og_hbm,
+    pin_ref,
+    pout_ref,
+    aux_ref,
+    query_ref,
+    out_ref,
+    act,
+    og,
+    part,
+    got,
+    mine,
+    gathered,
+    load_sem,
+    part_send,
+    part_recv,
+    dp_send,
+    dp_recv,
+):
+    layers = lax.axis_size("tensor")
+    pieces = lax.axis_size("dp")
+    ti = lax.axis_index("tensor")
+    di = lax.axis_index("dp")
+    rank = pin_ref.shape[1]
+    tokens = act.shape[1]
+    seq_len = tokens // ex_local
+    half = mine.shape[1]
+
+    loads = []
+    for d in range(1, layers + 1):
+        layer = lax.rem(ti + d, layers)
+        one = pltpu.make_async_copy(act_hbm.at[layer], act.at[d - 1], load_sem.at[2 * d - 2])
+        two = pltpu.make_async_copy(og_hbm.at[layer], og.at[d - 1], load_sem.at[2 * d - 1])
+        one.start()
+        two.start()
+        loads.append((one, two))
+
+    barrier = pltpu.get_barrier_semaphore()
+    for d in range(1, layers):
+        pl.semaphore_signal(
+            barrier, inc=1, device_id=(di, lax.rem(ti + d, layers)), device_id_type=MESH
+        )
+    for d in range(1, pieces):
+        pl.semaphore_signal(
+            barrier, inc=1, device_id=(lax.rem(di + d, pieces), ti), device_id_type=MESH
+        )
+    pl.semaphore_wait(barrier, layers - 1 + pieces - 1)
+
+    sends = []
+    for d in range(1, layers + 1):
+        layer = lax.rem(ti + d, layers)
+        loads[d - 1][0].wait()
+        loads[d - 1][1].wait()
+        in_part = dot_nt(act[d - 1], pin_ref[layer])
+        out_part = dot_nt(og[d - 1], pout_ref[layer])
+        gap = jnp.zeros((tokens, NB // 2 - rank), jnp.float32)
+        both = jnp.concatenate([in_part, gap, out_part, gap], axis=1).T
+        part[d - 1, 0:rank, :] = both[0:rank]
+        part[d - 1, rank : 2 * rank, :] = both[NB // 2 : NB // 2 + rank]
+        if d < layers:
+            copy = pltpu.make_async_remote_copy(
+                src_ref=part.at[d - 1],
+                dst_ref=got.at[d - 1],
+                send_sem=part_send.at[d - 1],
+                recv_sem=part_recv.at[d - 1],
+                device_id=(di, layer),
+                device_id_type=MESH,
+            )
+            copy.start()
+            sends.append(copy)
+    out_ref[...] = jnp.zeros_like(out_ref)
+    total_slots = ex_local * pieces
+    out_ref[total_slots : total_slots + query_ref.shape[0], 0:size] = query_ref[...]
+    total = part[layers - 1]
+    for d, copy in enumerate(sends):
+        copy.wait()
+        total = total + got[d]
+    in_rows = total[0:rank] * aux_ref[0:1, :]
+    out_rows = total[rank : 2 * rank]
+    grads = []
+    for s in range(ex_local):
+        lanes = slice(s * seq_len, (s + 1) * seq_len)
+        grads.append(
+            lax.dot_general(
+                out_rows[:, lanes],
+                in_rows[:, lanes],
+                (((1,), (1,)), ((), ())),
+                precision=lax.Precision.HIGHEST,
+                preferred_element_type=jnp.float32,
+            )
+        )
+    stacked = jnp.concatenate(grads, axis=0)
+    width = 2 * half
+    col = lax.broadcasted_iota(jnp.int32, (rank, width), 1)
+    row = lax.broadcasted_iota(jnp.int32, (rank, width), 0)
+    colf = col.astype(jnp.float32)
+    residue = colf - rank * jnp.floor((colf + 0.5) * (1.0 / rank))
+    place = jnp.where(residue == row.astype(jnp.float32), 1.0, 0.0).astype(jnp.bfloat16)
+    flat = None
+    for term in split3(stacked):
+        piece = jnp.dot(term, place, preferred_element_type=jnp.float32)
+        flat = piece if flat is None else flat + piece
+    keep = (col >= row * rank) & (col < row * rank + rank)
+    id_col = lax.broadcasted_iota(jnp.int32, (1, width), 1) == round_up(size, NB)
+    for s in range(ex_local):
+        slot = jnp.where(keep, flat[s * rank : (s + 1) * rank], 0.0)
+        line = jnp.sum(slot, axis=0, keepdims=True)
+        line = jnp.where(id_col, jnp.broadcast_to(aux_ref[1:2, s : s + 1], line.shape), line)
+        mine[s : s + 1, :] = line[:, 0:half]
+        mine[ex_local + s : ex_local + s + 1, :] = line[:, half:width]
+    copies = []
+    for d in range(1, pieces):
+        copy = pltpu.make_async_remote_copy(
+            src_ref=mine,
+            dst_ref=gathered.at[di],
+            send_sem=dp_send.at[d - 1],
+            recv_sem=dp_recv.at[d - 1],
+            device_id=(lax.rem(di + d, pieces), ti),
+            device_id_type=MESH,
+        )
+        copy.start()
+        copies.append(copy)
+    gathered[di] = mine[...]
+    for copy in copies:
+        copy.wait()
+    for p in range(pieces):
+        block = gathered[p]
+        out_ref[p * ex_local : (p + 1) * ex_local, 0:half] = block[0:ex_local]
+        out_ref[p * ex_local : (p + 1) * ex_local, half:width] = block[ex_local : 2 * ex_local]
+
+
+def project(activations, out_grads, proj_in, proj_out, lengths, example_ids, queries):
+    ex_local = lengths.shape[0]
+    layers, tokens, _ = activations.shape
+    rank = proj_in.shape[1]
+    size = rank * rank
     width = round_up(size, CB)
-    extra = CB
-    rows = width + extra
-    rhs = jnp.concatenate([grads, queries], axis=0)
-    rhs = jnp.pad(rhs, ((0, extra - slots - asked), (0, width - size)))
-    lead = jnp.pad(grads.T, ((0, rows - size), (0, NB - slots)))
-    lead = jnp.stack([lead, lead * (-1.0 / slots)])
-    out = pl.pallas_call(
-        functools.partial(solve_kernel, size),
-        out_shape=jax.ShapeDtypeStruct((extra, CB), jnp.float32),
+    pieces = lax.axis_size("dp")
+    seq_len = tokens // ex_local
+    live = (jnp.arange(seq_len, dtype=jnp.int32)[None, :] < lengths[:, None]).astype(jnp.float32)
+    ids = jnp.pad(example_ids.astype(jnp.float32), (0, tokens - ex_local))
+    aux = jnp.stack([live.reshape(tokens), ids])
+    return pl.pallas_call(
+        functools.partial(project_kernel, ex_local, size),
+        out_shape=jax.ShapeDtypeStruct((CB, width), jnp.float32),
+        in_specs=[pl.BlockSpec(memory_space=pl.ANY)] * 2
+        + [pl.BlockSpec(memory_space=pltpu.VMEM)] * 4,
+        out_specs=pl.BlockSpec(memory_space=pltpu.VMEM),
+        scratch_shapes=[
+            pltpu.VMEM(activations.shape, activations.dtype),
+            pltpu.VMEM(out_grads.shape, out_grads.dtype),
+            pltpu.VMEM((layers, 2 * rank, tokens), jnp.float32),
+            pltpu.VMEM((layers - 1, 2 * rank, tokens), jnp.float32),
+            pltpu.VMEM((2 * ex_local, width // 2), jnp.float32),
+            pltpu.VMEM((pieces, 2 * ex_local, width // 2), jnp.float32),
+            pltpu.SemaphoreType.DMA((2 * layers,)),
+            pltpu.SemaphoreType.DMA((layers - 1,)),
+            pltpu.SemaphoreType.DMA((layers - 1,)),
+            pltpu.SemaphoreType.DMA((pieces - 1,)),
+            pltpu.SemaphoreType.DMA((pieces - 1,)),
+        ],
+        compiler_params=pltpu.CompilerParams(
+            collective_id=0, has_side_effects=True, vmem_limit_bytes=48 * 1024 * 1024
+        ),
+    )(activations, out_grads, proj_in, proj_out, aux, queries)
+
+
+def solve_scores(prior, damping, rhs, slots, asked, ex_local):
+    size = prior.shape[0]
+    width = rhs.shape[1]
+    rows = width + rhs.shape[0]
+    return pl.pallas_call(
+        functools.partial(solve_kernel, size, slots, asked, ex_local),
+        out_shape=jax.ShapeDtypeStruct((ex_local, asked), jnp.float32),
         in_specs=[
             pl.BlockSpec(memory_space=pltpu.SMEM),
-            pl.BlockSpec(memory_space=pltpu.VMEM),
             pl.BlockSpec(memory_space=pltpu.VMEM),
             pl.BlockSpec(memory_space=pltpu.VMEM),
         ],
         out_specs=pl.BlockSpec(memory_space=pltpu.VMEM),
         scratch_shapes=[
             pltpu.VMEM((rows // CB, rows, CB), jnp.float32),
-            pltpu.VMEM((rows, 6 * NB), jnp.bfloat16),
-            pltpu.VMEM((rows, 6 * NB), jnp.bfloat16),
+            pltpu.VMEM((rows, TERMS * NB), jnp.bfloat16),
+            pltpu.VMEM((rows, TERMS * NB), jnp.bfloat16),
             pltpu.VMEM((NB, NB), jnp.float32),
         ],
         compiler_params=pltpu.CompilerParams(vmem_limit_bytes=56 * 1024 * 1024),
-    )(damping.reshape(1, 1), prior, rhs, lead)
-    return out[:slots, slots : slots + asked]
+    )(damping.reshape(1, 1), prior, rhs)
 
 
 def per_device(
     activations, out_grads, proj_in, proj_out, lengths, example_ids, prior_cov, damping, queries
 ):
     ex_local = lengths.shape[0]
-    rank = proj_in.shape[1]
-    seq_len = activations.shape[1] // ex_local
-    owner_index = lax.axis_index("tensor")
-    live_mask = (jnp.arange(seq_len, dtype=jnp.int32)[None, :] < lengths[:, None]).astype(
-        jnp.float32
+    slots = ex_local * lax.axis_size("dp")
+    rhs = project(
+        activations, out_grads, proj_in, proj_out, lengths, example_ids, queries[0]
     )
-    in_parts = jnp.einsum("ltf,lkf->ltk", activations, proj_in, preferred_element_type=jnp.float32)
-    out_parts = jnp.einsum("ltf,lkf->ltk", out_grads, proj_out, preferred_element_type=jnp.float32)
-    in_summed, out_summed = lax.psum((in_parts, out_parts), "tensor")
-    in_rows = lax.dynamic_index_in_dim(in_summed, owner_index, 0, keepdims=False)
-    out_rows = lax.dynamic_index_in_dim(out_summed, owner_index, 0, keepdims=False)
-    in_rows = in_rows.reshape(ex_local, seq_len, rank) * live_mask[:, :, None]
-    out_rows = out_rows.reshape(ex_local, seq_len, rank)
-    proj_grads = jnp.einsum(
-        "est,esu->etu", out_rows, in_rows, precision=lax.Precision.HIGHEST
-    ).reshape(ex_local, rank * rank)
-    ids = lax.all_gather(example_ids, "dp", axis=0, tiled=True)
-    piece_rows = lax.all_gather(proj_grads, "dp", axis=0, tiled=True)
-    scores = solve_scores(prior_cov[0], damping, queries[0], piece_rows)
-    mine = lax.axis_index("dp") * ex_local + jnp.arange(ex_local, dtype=jnp.int32)
-    pick = (ids[None, :] == mine[:, None]).astype(jnp.float32)
-    chosen = jnp.dot(pick, scores, precision=lax.Precision.HIGHEST)
+    chosen = solve_scores(prior_cov[0], damping, rhs, slots, queries.shape[1], ex_local)
     return lax.psum(chosen, "tensor")
 
 

time: 259 us -> 186 us (0.72)
  blocking collectives: 50.3 us -> 8.16 us
  waiting for transfers between devices: 21.5 us -> 0 us
  Pallas kernels: 150 us -> 171 us
  matrix products: 15.9 us -> 0 us
  between operations: 14.8 us -> 0.68 us
    all_gather x1 -> x0, blocking collectives: 30.7 us -> none  [per_device(): piece_rows = lax.all_gather(proj_grads, 'dp', axis=0, tiled=True)]
    psum x1 -> x0, waiting for transfers between devices: 21.5 us -> none  [per_device(): in_summed, out_summed = lax.psum((in_parts, out_parts), 'tensor')]
    pallas_call x1 -> x2, Pallas kernels: 150 us -> 171 us  [the longest x1 150 us: solve_scores(): pl.pallas_call(functools.partial(solve_kernel, size, slots, asked, ex_loc...]
    dot_general x4 -> x0, matrix products: 15.9 us -> none  [the longest x1 10.3 us: per_device(): jnp.einsum('ltf,lkf->ltk', activations, proj_in, preferred_element_type=j...]
    unnamed x1 -> x0, blocking collectives: 13.1 us -> none
    unnamed x17 -> x8, local copies, waits for them, and re-layouts: 1.9 us -> 4.49 us
  transfers between devices with their start and end apart: 1 -> 0, of which waited for: 1 -> 0; matrix products, arithmetic and copies ran while one was open for 0% -> 0% of each run, Pallas kernels for 0% -> 0%
where the time goes in v2:
time: 186 us
  Pallas kernels  171 us (92%)
  blocking collectives  8.16 us (4%)
  local copies, waits for them, and re-layouts  4.49 us (2%)
    pallas_call x1, Pallas kernels, solve_scores(): pl.pallas_call(functools.partial(solve_kernel, size, slots, asked, ex_loc...  150 us
    pallas_call x1, Pallas kernels, project(): pl.pallas_call(functools.partial(project_kernel, ex_local, size), out_sha...  21.3 us
    psum x1, blocking collectives, per_device(): return lax.psum(chosen, 'tensor')  8.16 us
    unnamed x8, local copies, waits for them, and re-layouts  4.49 us

profile of v2, /device:TPU:0, one launch (start us, length us, event | category | flops | bytes accessed | tf_op | source)
XLA Modules:
  0.0 186.1 jit_solution(5789946445572235903)
XLA Ops:
  0.0 0.7 convert_element_type.20
  0.7 0.7 fusion
  1.4 0.0 copy-start.1
  1.4 1.2 copy-done.1
  2.7 0.0 copy-start.2
  2.7 1.0 copy-done.2
  3.7 0.0 copy-start.3
  3.7 1.0 copy-done.3
  4.6 21.3 %shard_map.91.rhs_ref = f32[256,1792]{1,0:T(8,128)S(1)} custom-call(bf16[4,512,3584]{2,1,0:T(8,128)(2,1)} %act_hbm.1, bf16[4,512,1024]{2,1,0:T(8,128)(2,1)} %og_hbm.1, bf16[4,40,3584]{2,1,0:T(8,128)(2,1)S(1)} %copy-done.1, bf16[4,40,1024]{2,1,0:T(8,128)(2,1)S(1)} %copy-done.3, f32[2,512]{1,0:T(2,128)S(1)} %pad_maximum_fusion.aux_ref, f32[64,1600]{1,0:T(8,128)S(1)} %bitcast.6), custom_call_target="tpu_custom_call" | custom-call | tf_op jit(solution)/shard_map/pallas_call | solution.py:318
  26.0 0.0 copy-start
  26.0 1.3 copy-done
  27.9 150.1 %shard_map.92 = f32[4,64]{1,0:T(4,128)} custom-call(f32[1,1]{1,0:T(1,128)} %bitcast.5.damping_ref, bf16[1600,1600]{1,0:T(8,128)(2,1)} %bitcast.7, f32[256,1792]{1,0:T(8,128)} %copy-done), custom_call_target="tpu_custom_call" | custom-call | tf_op jit(solution)/shard_map/pallas_call | solution.py:347
  178.0 8.2 %psum.7 = f32[4,64]{1,0:T(4,128)} all-reduce(f32[4,64]{1,0:T(4,128)} %shard_map.92), channel_id=1, replica_groups=mesh['dp'=8,'tensor'=4] {'tensor'}, use_global_device_ids=true, to_apply=%region_0.1 | all-reduce | flops 256 | bytes 2048 | tf_op jit(solution)/shard_map/psum | solution.py:375
  (2 shorter events, 0.0 us)
Async XLA Ops:
  1.4 1.3 copy-start.1
  2.7 1.0 copy-start.2
  3.7 1.0 copy-start.3
  26.0 1.3 copy-start

commit v3 on v2

--- a/solution.py
+++ b/solution.py
@@ -10,7 +10,7 @@
 MESH = pl.DeviceIdType.MESH
 NB = 128
 CB = 256
-TERMS = 6
+TERMS = 4
 
 
 def round_up(value, step):
@@ -25,14 +25,19 @@
     return high, mid, low
 
 
+def split2(x):
+    high = x.astype(jnp.bfloat16)
+    return high, (x - high.astype(jnp.float32)).astype(jnp.bfloat16)
+
+
 def stack_left(x):
-    h, m, l = split3(x)
-    return jnp.concatenate([h, h, m, h, l, m], axis=1)
+    h, m = split2(x)
+    return jnp.concatenate([h, m, h, m], axis=1)
 
 
 def stack_right(x):
-    h, m, l = split3(x)
-    return jnp.concatenate([h, m, h, l, h, m], axis=1)
+    h, m = split2(x)
+    return jnp.concatenate([h, h, m, m], axis=1)
 
 
 def dot_nt(a, b):
@@ -43,42 +48,70 @@
     return jnp.broadcast_to(row, shape)
 
 
-def invert_block(rows):
+def invert_eight(cols):
+    sub = lax.broadcasted_iota(jnp.int32, (8, NB), 0)
+    for p in range(0, 8, 2):
+        q = p + 1
+        at_p, at_q = sub == p, sub == q
+        first, second = cols[p], cols[q]
+        a = across(first[p : p + 1, :])
+        b = across(second[p : p + 1, :])
+        c = across(second[q : q + 1, :])
+        inv = 1.0 / (a * c - b * b)
+        new = []
+        for j in range(8):
+            if j == p:
+                new.append(jnp.where(at_p, c, jnp.where(at_q, -b, second * b - first * c)) * inv)
+            elif j == q:
+                new.append(jnp.where(at_p, -b, jnp.where(at_q, a, first * b - second * a)) * inv)
+            else:
+                u = across(cols[j][p : p + 1, :])
+                v = across(cols[j][q : q + 1, :])
+                x = c * u - b * v
+                y = a * v - b * u
+                change = jnp.where(at_p, -x, jnp.where(at_q, -y, first * x + second * y))
+                new.append(jnp.where(at_p | at_q, 0.0, cols[j]) - change * inv)
+        cols = new
+    return cols
+
+
+def tree_sum(terms):
+    while len(terms) > 1:
+        terms = [terms[i] + terms[i + 1] for i in range(0, len(terms), 2)]
+    return terms[0]
+
+
+def invert_block(rows, between):
     sub = lax.broadcasted_iota(jnp.int32, (8, NB), 0)
     lane = lax.broadcasted_iota(jnp.int32, (8, NB), 1)
     count = len(rows)
+    diagonal = [jnp.where(lane == sub + 8 * i, rows[i], 0.0) for i in range(count)]
+    along = lax.rsqrt(across(jnp.sum(tree_sum(diagonal), axis=0, keepdims=True)))
+    down = [
+        lax.rsqrt(jnp.broadcast_to(jnp.sum(d, axis=1, keepdims=True), (8, NB))) for d in diagonal
+    ]
+    rows = [rows[i] * down[i] * along for i in range(count)]
     for kb in range(count):
         base = 8 * kb
         strip = rows[kb]
-        cols = [across(strip[:, base + j : base + j + 1]) for j in range(8)]
-        for p in range(8):
-            pivot_col = cols[p]
-            inv = 1.0 / across(pivot_col[p : p + 1, :])
-            new = []
-            for j in range(8):
-                if j == p:
-                    new.append(jnp.where(sub == p, inv, -pivot_col * inv))
-                else:
-                    lead = across(cols[j][p : p + 1, :])
-                    new.append(jnp.where(sub == p, lead * inv, cols[j] - (pivot_col * lead) * inv))
-            cols = new
+        cols = invert_eight([across(strip[:, base + j : base + j + 1]) for j in range(8)])
         inside = (lane >= base) & (lane < base + 8)
         strip = jnp.where(inside, jnp.where(lane - base == sub, 1.0, 0.0), strip)
-        terms = [cols[j] * across(strip[j : j + 1, :]) for j in range(8)]
-        top = ((terms[0] + terms[1]) + (terms[2] + terms[3])) + (
-            (terms[4] + terms[5]) + (terms[6] + terms[7])
-        )
+        top = tree_sum([cols[j] * across(strip[j : j + 1, :]) for j in range(8)])
         spread = [across(top[j : j + 1, :]) for j in range(8)]
         for step in range(1, count):
             i = (kb + step) % count
             row = rows[i]
             parts = [across(row[:, base + j : base + j + 1]) * spread[j] for j in range(8)]
-            total = ((parts[0] + parts[1]) + (parts[2] + parts[3])) + (
-                (parts[4] + parts[5]) + (parts[6] + parts[7])
-            )
-            rows[i] = jnp.where(inside, 0.0, row) - total
+            rows[i] = jnp.where(inside, 0.0, row) - tree_sum(parts)
         rows[kb] = top
-    return rows
+        between()
+    return [rows[i] * down[i] * along for i in range(count)]
+
+
+def tiles_each(k, all_blocks):
+    rest = all_blocks - 1 - (k + 1) // 2
+    return -(-(rest * (rest + 1) // 2) // (NB // 8))
 
 
 def solve_kernel(
@@ -112,18 +145,17 @@
         mat[jj, width:, :] = rhs_ref[:, jj * CB : (jj + 1) * CB]
     mat[col_blocks, width:, :] = jnp.zeros((mat.shape[1] - width, CB), jnp.float32)
 
-    def trail(first):
-        def per_col(jj, carry):
-            weights = right[pl.ds(pl.multiple_of(jj * CB, CB), CB), :]
-
-            def per_row(r, inner):
-                at = pl.multiple_of(r * CB, CB)
-                mat[jj, pl.ds(at, CB), :] -= dot_nt(left[pl.ds(at, CB), :], weights)
-                return inner
-
-            return lax.fori_loop(jj, all_blocks, per_row, carry)
-
-        lax.fori_loop(first, all_blocks, per_col, 0)
+    def tile(jj, r):
+        at = pl.multiple_of(r * CB, CB)
+        weights = right[pl.ds(pl.multiple_of(jj * CB, CB), CB), :]
+        mat[jj, pl.ds(at, CB), :] -= dot_nt(left[pl.ds(at, CB), :], weights)
+
+    def update_col(jj):
+        def per_row(r, carry):
+            tile(jj, r)
+            return carry
+
+        lax.fori_loop(jj, all_blocks, per_row, 0)
 
     live = lax.broadcasted_iota(jnp.int32, (NB, CB), 0) < slots
     for jj in range(col_blocks):
@@ -132,30 +164,59 @@
         left[jj * CB : (jj + 1) * CB, :] = stack_left(piece * (-1.0 / slots))
     right[width:, :] = jnp.zeros((mat.shape[1] - width, TERMS * NB), jnp.bfloat16)
     left[width:, :] = jnp.zeros((mat.shape[1] - width, TERMS * NB), jnp.bfloat16)
-    trail(0)
-
-    def step(k, carry):
+    def panels(k):
         half = k // 2
         lanes = pl.ds(pl.multiple_of((k % 2) * NB, NB), NB)
-        top = pl.multiple_of(k * NB, NB)
-        rows = [mat[half, pl.ds(top + 8 * i, 8), lanes] for i in range(NB // 8)]
-        rows = invert_block(rows)
-        for i in range(NB // 8):
-            dinv[8 * i : 8 * i + 8, :] = rows[i]
         inverse = stack_right(dinv[...])
 
-        def per_row(r, inner):
+        def per_row(r, carry):
             at = pl.multiple_of(r * CB, CB)
             panel = mat[half, pl.ds(at, CB), lanes]
             right[pl.ds(at, CB), :] = stack_right(panel)
             left[pl.ds(at, CB), :] = stack_left(dot_nt(stack_left(panel), inverse))
-            return inner
+            return carry
 
         lax.fori_loop(half, all_blocks, per_row, 0)
-        trail((k + 1) // 2)
+
+    def step(each, k, carry):
+        @pl.when(k >= 0)
+        def _():
+            panels(k)
+
+        later = k + 1
+        half = later // 2
+        update_col(half)
+        lanes = pl.ds(pl.multiple_of((later % 2) * NB, NB), NB)
+        top = pl.multiple_of(later * NB, NB)
+        rows = [mat[half, pl.ds(top + 8 * i, 8), lanes] for i in range(NB // 8)]
+        place = [half + 1, half + 1]
+
+        def between():
+            for _ in range(each):
+                jj, r = place
+                left_over = jj < all_blocks
+                tile(jnp.where(left_over, jj, all_blocks - 1), jnp.where(left_over, r, 0))
+                wrap = r + 1 >= all_blocks
+                place[0] = jnp.where(wrap, jj + 1, jj)
+                place[1] = jnp.where(wrap, jj + 1, r + 1)
+
+        rows = invert_block(rows, between)
+        for i in range(NB // 8):
+            dinv[8 * i : 8 * i + 8, :] = rows[i]
         return carry
 
-    lax.fori_loop(0, round_up(size, NB) // NB, step, 0)
+    blocks = round_up(size, NB) // NB
+    start = -1
+    while start < blocks - 1:
+        each = tiles_each(start, all_blocks)
+        stop = start
+        while stop < blocks - 1 and tiles_each(stop, all_blocks) == each:
+            stop += 1
+        lax.fori_loop(start, stop, functools.partial(step, each), 0)
+        start = stop
+    panels(blocks - 1)
+    for jj in range(blocks // 2, all_blocks):
+        update_col(jj)
     id_at = round_up(size, NB)
     ids = jnp.broadcast_to(rhs_ref[0:slots, id_at : id_at + 1], (slots, NB))
     own = lax.broadcasted_iota(jnp.int32, (slots, NB), 1) + lax.axis_index("dp") * ex_local

time: 186 us -> 136 us (0.73)
  Pallas kernels: 171 us -> 121 us
    pallas_call x1, Pallas kernels: 150 us -> 99.8 us  [solve_scores(): pl.pallas_call(functools.partial(solve_kernel, size, slots, asked, ex_loc...]
where the time goes in v3:
time: 136 us
  Pallas kernels  121 us (89%)
  blocking collectives  8.17 us (6%)
  local copies, waits for them, and re-layouts  4.49 us (3%)
  other arithmetic  1.39 us (1%)
    pallas_call x1, Pallas kernels, solve_scores(): pl.pallas_call(functools.partial(solve_kernel, size, slots, asked, ex_loc...  99.8 us
    pallas_call x1, Pallas kernels, project(): pl.pallas_call(functools.partial(project_kernel, ex_local, size), out_sha...  21.3 us
    psum x1, blocking collectives, per_device(): return lax.psum(chosen, 'tensor')  8.17 us
    unnamed x8, local copies, waits for them, and re-layouts  4.49 us

profile of v3, /device:TPU:0, one launch (start us, length us, event | category | flops | bytes accessed | tf_op | source)
XLA Modules:
  0.0 135.8 jit_solution(12999999482248609585)
XLA Ops:
  0.0 0.7 convert_element_type.20
  0.7 0.7 fusion
  1.4 0.0 copy-start.1
  1.4 1.2 copy-done.1
  2.7 0.0 copy-start.2
  2.7 1.0 copy-done.2
  3.7 0.0 copy-start.3
  3.7 1.0 copy-done.3
  4.6 21.3 %shard_map.91.rhs_ref = f32[256,1792]{1,0:T(8,128)S(1)} custom-call(bf16[4,512,3584]{2,1,0:T(8,128)(2,1)} %act_hbm.1, bf16[4,512,1024]{2,1,0:T(8,128)(2,1)} %og_hbm.1, bf16[4,40,3584]{2,1,0:T(8,128)(2,1)S(1)} %copy-done.1, bf16[4,40,1024]{2,1,0:T(8,128)(2,1)S(1)} %copy-done.3, f32[2,512]{1,0:T(2,128)S(1)} %pad_maximum_fusion.aux_ref, f32[64,1600]{1,0:T(8,128)S(1)} %bitcast.6), custom_call_target="tpu_custom_call" | custom-call | tf_op jit(solution)/shard_map/pallas_call | solution.py:379
  26.0 0.0 copy-start
  26.0 1.3 copy-done
  27.9 99.8 %shard_map.92 = f32[4,64]{1,0:T(4,128)} custom-call(f32[1,1]{1,0:T(1,128)} %bitcast.5.damping_ref, bf16[1600,1600]{1,0:T(8,128)(2,1)} %bitcast.7, f32[256,1792]{1,0:T(8,128)} %copy-done), custom_call_target="tpu_custom_call" | custom-call | tf_op jit(solution)/shard_map/pallas_call | solution.py:408
  127.6 8.2 %psum.7 = f32[4,64]{1,0:T(4,128)} all-reduce(f32[4,64]{1,0:T(4,128)} %shard_map.92), channel_id=1, replica_groups=mesh['dp'=8,'tensor'=4] {'tensor'}, use_global_device_ids=true, to_apply=%region_0.1 | all-reduce | flops 256 | bytes 2048 | tf_op jit(solution)/shard_map/psum | solution.py:436
  (2 shorter events, 0.0 us)
Async XLA Ops:
  1.4 1.3 copy-start.1
  2.7 1.0 copy-start.2
  3.7 1.0 copy-start.3
  26.0 1.3 copy-start
